TPU v7x, 256 devices: a whole 4x4x8 slice. The times are simulated.
256 devices in a mesh: seq: 64 (over y, x_lo, z), head: 4 (over x_hi, core).
Axes of the slice: x: 4 (x_hi: 2, x_lo: 2; x = x_hi * 2 + x_lo), y: 4, z: 8, core: 2. Of those that a mesh axis runs over, the one named last changes fastest.
Arguments:
- queries: bfloat16 [16384, 32, 128], P('seq', 'head'), may hold values from -6 to 6, as said below
- key_states: bfloat16 [16384, 4, 128], P('seq', 'head'), may hold values from -6 to 6, as said below
- value_vectors_all: bfloat16 [16384, 4, 128], P('seq', 'head'), may hold values from -6 to 6
- out_weight: bfloat16 [4096, 4096], P('head'), may hold values from -0.125 to 0.125
Outputs:
- mixed: bfloat16 [16384, 4096], P('seq', 'head')
Inputs may be any that keep to these rules, and one draw needn't show every extreme that they name: `queries`: query vectors; entries of order one. `key_states`: key vectors; entries of order one.
All inputs are finite; a program needn't handle non-finite values.
Results may differ from a plain program's by a relative error of at most 0.015.
Values may be sent and summed in bfloat16 or wider, within the bound.
No kernel may reach another device: no remote copies, remote signals or barrier semaphores. Data moves between devices by JAX's collectives and lax.ppermute only.
A program may use at most 64 MiB of HBM per device.

v0:
```python
import functools
import math

import jax
import jax.numpy as jnp
from jax import lax
from jax.experimental import pallas as pl
from jax.experimental.pallas import tpu as pltpu
from jax.sharding import PartitionSpec as P

NY, NX, NZ = 4, 2, 8
TOK = 256
HEADS = 8
HD = 128
ROWS = TOK * HEADS
DEEP = HD + 16
SLOTS = NY * NZ
KEYS = SLOTS * TOK
KT = 1024
RC = 512
PER_TILE = KT // TOK
SCALE2 = math.log2(math.e) / math.sqrt(HD)
LOW, HIGH = 1e-20, 1e34
NEG = -1e30
AXES = ("seq", "head")
BOTH = (((1,), (1,)), ((), ()))


def device(X, y, x, z, c):
    return ((y % NY) * 16 + x * 8 + z % NZ) * 4 + X * 2 + c


def perm_of(f):
    return [
        (device(X, y, x, z, c), device(*f(X, y, x, z, c)))
        for y in range(NY)
        for x in range(NX)
        for z in range(NZ)
        for X in range(2)
        for c in range(2)
    ]


def sign_of(pos, c):
    return 1 - 2 * ((pos + c) % 2)


SWAP = perm_of(lambda X, y, x, z, c: (X, y, x, z, c) if c == x else (X, 3 - y, 1 - x, z, 1 - c))
SWAP_BACK = [pair for pair in SWAP if pair[0] != pair[1]]
CORE = perm_of(lambda X, y, x, z, c: (X, y, x, z, 1 - c))
XHI = perm_of(lambda X, y, x, z, c: (1 - X, y, x, z, c))
Z_NEAR = perm_of(lambda X, y, x, z, c: (X, y, x, z + sign_of(z, c), c))
Z_FAR = perm_of(lambda X, y, x, z, c: (X, y, x, z - sign_of(z, c), c))
Z_SKIP = perm_of(lambda X, y, x, z, c: (X, y, x, z + 2 * sign_of(z, c), c))
Y_NEAR = perm_of(lambda X, y, x, z, c: (X, y + sign_of(y, c), x, z, c))
Y_FAR = perm_of(lambda X, y, x, z, c: (X, y - sign_of(y, c), x, z, c))


def send(value, perm):
    return lax.ppermute(value, AXES, perm)


def score(k, q):
    return lax.dot_general(k, q, BOTH, preferred_element_type=jnp.float32) * SCALE2


def mask_tile(s, aheads):
    key = lax.broadcasted_iota(jnp.int32, (TOK, RC), 0)
    tok = lax.broadcasted_iota(jnp.int32, (TOK, RC), 1) % TOK
    parts = []
    for i, ahead in enumerate(aheads):
        parts.append(jnp.where(key <= tok + ahead, s[i * TOK : (i + 1) * TOK, :], NEG))
    return jnp.concatenate(parts, axis=0)


def fast_tile(q_ref, k_ref, v_ref, acc, block, t, aheads):
    k, v = k_ref[t], v_ref[t]
    s = score(k, q_ref[block, :RC, :])
    for r in range(0, ROWS, RC):
        if aheads is not None:
            s = mask_tile(s, aheads)
        p = jnp.exp2(s).astype(jnp.bfloat16)
        if r + RC < ROWS:
            s = score(k, q_ref[block, r + RC : r + 2 * RC, :])
        acc[block, :, r : r + RC] += jnp.dot(v, p, preferred_element_type=jnp.float32)


def slow_tile(q_ref, k_ref, v_ref, acc, top, block, t, aheads):
    def chunk(r, _):
        at = pl.ds(pl.multiple_of(r * RC, RC), RC)
        s = mask_tile(score(k_ref[t], q_ref[block, at, :]), aheads)
        old = top[:1, at]
        new = jnp.maximum(old, jnp.max(s, axis=0, keepdims=True))
        p = jnp.exp2(s - new).astype(jnp.bfloat16)
        sums = jnp.dot(v_ref[t], p, preferred_element_type=jnp.float32)
        acc[block, :, at] = acc[block, :, at] * jnp.exp2(old - new) + sums
        top[:, at] = jnp.broadcast_to(new, (8, RC))
        return 0

    lax.fori_loop(0, ROWS // RC, chunk, 0)


def tiles(run, info, rows, zs, first, n_tiles, base, block, split):
    def step(t, _):
        at = (first + t) * PER_TILE
        row = rows[first + t]
        nearest = zs[at]
        for i in range(1, PER_TILE):
            nearest = jnp.minimum(nearest, zs[at + i])
        whole = row < info[block]
        part = jnp.logical_and(row == info[2 + block], nearest <= info[4])
        aheads = [(info[4] - zs[at + i]) * TOK for i in range(PER_TILE)]
        if split:
            pl.when(whole)(lambda: run(base + t, None))
            pl.when(part)(lambda: run(base + t, aheads))
        else:
            aheads = [jnp.where(whole, TOK, ahead) for ahead in aheads]
            pl.when(jnp.logical_or(whole, part))(lambda: run(base + t, aheads))
        return 0

    lax.fori_loop(0, n_tiles, step, 0)


def place(piece, k_ref, v_ref, t):
    for i in range(PER_TILE):
        src, dst = 2 * i * TOK, i * TOK
        k_ref[t, dst : dst + TOK, :] = piece[src : src + TOK, :]
        for j in range(0, TOK, HD):
            values = piece[src + TOK + j : src + TOK + j + HD, :]
            v_ref[t, :HD, dst + j : dst + j + HD] = values
    v_ref[t, HD:, :] = jnp.ones((DEEP - HD, KT), jnp.bfloat16)


def fast_blocks(info, rows, zs, first, n_tiles, base, q_ref, k_ref, v_ref, acc):
    def block_step(block, _):
        def run(t, aheads):
            fast_tile(q_ref, k_ref, v_ref, acc, block, t, aheads)

        tiles(run, info, rows, zs, first, n_tiles, base, block, True)
        return 0

    lax.fori_loop(0, 2, block_step, 0)


def piece_kernel(first, n_tiles, has_state, info, rows, zs, q_ref, *refs):
    pieces, refs = refs[:n_tiles], refs[n_tiles:]
    acc, k_ref, v_ref = refs[-3:]
    if not has_state:
        acc[...] = jnp.zeros_like(acc)
    for t, piece in enumerate(pieces):
        place(piece, k_ref, v_ref, t)
    fast_blocks(info, rows, zs, first, n_tiles, 0, q_ref, k_ref, v_ref, acc)


def tile_scratch(n):
    return [pltpu.VMEM((n, KT, HD), jnp.bfloat16), pltpu.VMEM((n, DEEP, KT), jnp.bfloat16)]


VMEM = pl.BlockSpec(memory_space=pltpu.VMEM)
SMEM = pl.BlockSpec(memory_space=pltpu.SMEM)
STATE = jax.ShapeDtypeStruct((2, DEEP, ROWS), jnp.float32)
PART = jax.ShapeDtypeStruct((DEEP, ROWS), jnp.float32)


def cost(n_tiles):
    return pl.CostEstimate(
        flops=8 * n_tiles * ROWS * KT * HD,
        bytes_accessed=4 * 2**20,
        transcendentals=n_tiles * ROWS * KT,
    )


def attend_pieces(info, rows, zs, q, pieces, first, state=None):
    n_tiles = len(pieces)
    extra = [] if state is None else [state]
    return pl.pallas_call(
        functools.partial(piece_kernel, first, n_tiles, state is not None),
        out_shape=STATE,
        in_specs=[SMEM, SMEM, SMEM, VMEM] + [VMEM] * (n_tiles + len(extra)),
        out_specs=VMEM,
        scratch_shapes=tile_scratch(n_tiles),
        compiler_params=pltpu.CompilerParams(vmem_limit_bytes=20 * 2**20),
        input_output_aliases={} if state is None else {4 + n_tiles: 0},
        cost_estimate=cost(n_tiles),
        name=f"attend_{first}",
    )(info, rows, zs, q, *pieces, *extra)


def last_kernel(n_pieces, info, rows, zs, q_ref, state, *refs):
    pieces = refs[:n_pieces]
    acc, keep_ref, give_ref, k_ref, v_ref, top = refs[n_pieces:]
    last = n_pieces - 1
    place(pieces[last], k_ref, v_ref, last)
    fast_blocks(info, rows, zs, last, 1, last, q_ref, k_ref, v_ref, acc)
    for block, out_ref in enumerate((keep_ref, give_ref)):
        total = acc[block, HD : HD + 8, :]
        bad = jnp.logical_not(jnp.logical_and(total >= LOW, total <= HIGH))
        n_bad = jnp.sum(jnp.max(bad.astype(jnp.float32), axis=0, keepdims=True))
        some = jnp.logical_or(info[block] > 0, info[2 + block] >= 0)
        out_ref[HD + 8 :, :] = jnp.full((8, ROWS), jnp.where(some, 0.0, NEG), jnp.float32)

        @pl.when(jnp.logical_and(some, n_bad > 0.0))
        def _(block=block, out_ref=out_ref):
            acc[block] = jnp.zeros((DEEP, ROWS), jnp.float32)
            top[...] = jnp.full((8, ROWS), NEG, jnp.float32)
            for t, piece in enumerate(pieces[:last]):
                place(piece, k_ref, v_ref, t)

            def run(t, aheads):
                slow_tile(q_ref, k_ref, v_ref, acc, top, block, t, aheads)

            tiles(run, info, rows, zs, 0, n_pieces, 0, block, False)
            out_ref[HD + 8 :, :] = top[...]

        out_ref[: HD + 8, :] = acc[block, : HD + 8, :]


def attend_last(info, rows, zs, q, state, pieces):
    return pl.pallas_call(
        functools.partial(last_kernel, len(pieces)),
        out_shape=(STATE, PART, PART),
        in_specs=[SMEM, SMEM, SMEM] + [VMEM] * (2 + len(pieces)),
        out_specs=(VMEM, VMEM, VMEM),
        scratch_shapes=tile_scratch(len(pieces)) + [pltpu.VMEM((8, ROWS), jnp.float32)],
        input_output_aliases={4: 0},
        compiler_params=pltpu.CompilerParams(vmem_limit_bytes=20 * 2**20),
        cost_estimate=cost(1),
        name="attend_last",
    )(info, rows, zs, q, state, *pieces)[1:]


def merge_kernel(a_ref, b_ref, out_ref):
    sums, tops = slice(HD, HD + 1), slice(HD + 8, HD + 9)
    top = jnp.maximum(a_ref[tops, :], b_ref[tops, :])
    fa, fb = jnp.exp2(a_ref[tops, :] - top), jnp.exp2(b_ref[tops, :] - top)
    total = a_ref[sums, :] * fa + b_ref[sums, :] * fb
    fa, fb = fa / total, fb / total
    for h in range(HEADS):
        at = slice(h * TOK, (h + 1) * TOK)
        value = a_ref[:HD, at] * fa[:, at] + b_ref[:HD, at] * fb[:, at]
        out_ref[:, h * HD : (h + 1) * HD] = value.T.astype(jnp.bfloat16)


def merge(a, b):
    return pl.pallas_call(
        merge_kernel,
        out_shape=jax.ShapeDtypeStruct((TOK, HEADS * HD), jnp.bfloat16),
        in_specs=[VMEM, VMEM],
        out_specs=VMEM,
        compiler_params=pltpu.CompilerParams(vmem_limit_bytes=8 * 2**20),
        name="merge",
    )(a, b)


def pack_kernel(k_ref, v_ref, out_ref):
    out_ref[:TOK, :] = k_ref[...]
    for j in range(0, TOK, HD):
        out_ref[TOK + j : TOK + j + HD, :] = v_ref[j : j + HD, :].T


def pack(k, v):
    return pl.pallas_call(
        pack_kernel, out_shape=jax.ShapeDtypeStruct((2 * TOK, HD), jnp.bfloat16), name="pack"
    )(k, v)


COLS = 512
SLICE = 1024


def load_kernel(first, info, w_ref, out_ref, sem):
    col = pl.multiple_of(info[first] * SLICE, SLICE)
    copy = pltpu.make_async_copy(w_ref.at[:, pl.ds(col, 2 * SLICE)], out_ref, sem)
    copy.start()
    copy.wait()


def load_columns(info, w, first):
    return pl.pallas_call(
        functools.partial(load_kernel, first),
        out_shape=jax.ShapeDtypeStruct((w.shape[0], 2 * SLICE), w.dtype),
        in_specs=[SMEM, pl.BlockSpec(memory_space=pltpu.HBM)],
        out_specs=VMEM,
        scratch_shapes=[pltpu.SemaphoreType.DMA],
        compiler_params=pltpu.CompilerParams(vmem_limit_bytes=4 * 2**20),
        cost_estimate=pl.CostEstimate(flops=0, bytes_accessed=2**23, transcendentals=0),
        name=f"load_{first}",
    )(info, w)


def project_kernel(info, home_ref, away_ref, w_ref, give_ref, keep_ref, x_ref):
    x_ref[...] = home_ref[...]

    @pl.when(info[5] == 0)
    def _():
        x_ref[...] = away_ref[...]

    for out_ref, side in ((give_ref, 1 - info[6]), (keep_ref, info[6])):
        for j in range(0, SLICE, COLS):
            at = pl.ds(pl.multiple_of(side * SLICE + j, COLS), COLS)
            value = jnp.dot(x_ref[...], w_ref[:, at], preferred_element_type=jnp.float32)
            out_ref[:, j : j + COLS] = value.astype(out_ref.dtype)


def project(info, home, away, w):
    return pl.pallas_call(
        project_kernel,
        out_shape=(
            jax.ShapeDtypeStruct((TOK, SLICE), jnp.bfloat16),
            jax.ShapeDtypeStruct((TOK, SLICE), jnp.float32),
        ),
        in_specs=[SMEM, VMEM, VMEM, VMEM],
        out_specs=(VMEM, VMEM),
        scratch_shapes=[pltpu.VMEM((TOK, SLICE), jnp.bfloat16)],
        compiler_params=pltpu.CompilerParams(vmem_limit_bytes=8 * 2**20),
        name="project",
    )(info, home, away, w)


def on_device(queries, key_states, value_vectors_all, out_weight):
    seq = lax.axis_index("seq")
    head = lax.axis_index("head")
    y, x, z = seq // 16, (seq // 8) % 2, seq % 8
    X, c = head // 2, head % 2
    diagonal = c == x

    k = key_states.reshape(TOK, HD)
    v = value_vectors_all.reshape(TOK, HD)
    kv = send(pack(k, v), SWAP)
    q = queries.transpose(1, 0, 2).reshape(ROWS, HD)

    sz, sy = sign_of(z, c), sign_of(y, c)
    near_z, far_z, skip_z = send(kv, Z_NEAR), send(kv, Z_FAR), send(kv, Z_SKIP)
    near_z, far_z, skip_z, q = lax.optimization_barrier((near_z, far_z, skip_z, q))
    q_own = send(q, SWAP)
    side = jnp.concatenate([far_z, skip_z], axis=0)
    a = jnp.concatenate([kv, near_z, side], axis=0)
    a_near, a_far = send(a, Y_NEAR), send(a, Y_FAR)
    b = jnp.concatenate([send(side, Z_NEAR), send(side, Z_SKIP)], axis=0)
    b_near, b_far = send(b, Y_NEAR), send(b, Y_FAR)
    a_near, b = lax.optimization_barrier((a_near, b))
    a_last = send(a_near, Y_FAR)
    q_own, b = lax.optimization_barrier((q_own, b))
    q_other = send(q_own, CORE)

    def block_row(chip_y):
        return jnp.where(diagonal, chip_y % NY, NY - 1 - chip_y % NY)

    own_row = block_row(y)
    other_rows = NY - 1 - own_row + jnp.where(c == 0, 1, 0)
    info = jnp.stack([own_row, other_rows, own_row, jnp.int32(-1), z, diagonal, c, 2 * X, 2 - 2 * X]).astype(jnp.int32)
    near, far, last = block_row(y + sy), block_row(y - sy), block_row(y - 2 * sy)
    rows = jnp.stack([own_row, near, far, own_row, near, last, far, last]).astype(jnp.int32)
    z_a = [z, z + sz, z - sz, z - 2 * sz]
    z_b = [z + 2 * sz, z + 3 * sz, z - 3 * sz, z - 4 * sz]
    zs = jnp.stack([w % NZ for w in z_a * 3 + z_b * 2 + z_a + z_b * 2]).astype(jnp.int32)
    q = jnp.stack([q_own, q_other])

    early = [a, a_near, a_far]
    state = attend_pieces(info, rows, zs, q, lax.optimization_barrier((early, b))[0], 0)
    b_near, state = lax.optimization_barrier((b_near, state))
    b_last = send(b_near, Y_FAR)
    middle = [b, b_near, a_last, b_far]
    state = attend_pieces(info, rows, zs, q, middle, 3, state)
    pieces = early + middle + [b_last]
    keep, give = attend_last(info, rows, zs, q, state, pieces)
    home = merge(keep, send(give, CORE))
    home, out_weight = lax.optimization_barrier((home, out_weight))
    w_far = load_columns(info, out_weight, 8)
    away = send(home, SWAP_BACK)

    far_give, far_keep = project(info, home, away, w_far)
    far = (far_keep + send(far_give, CORE).astype(jnp.float32)).astype(jnp.bfloat16)
    home, out_weight, far = lax.optimization_barrier((home, out_weight, far))
    far = send(far, XHI)
    near_give, near_keep = project(info, home, away, load_columns(info, out_weight, 7))
    near = near_keep + send(near_give, CORE).astype(jnp.float32)
    return (near + far.astype(jnp.float32)).astype(jnp.bfloat16)


def solution(mesh):
    in_specs = (
        P("seq", "head", None),
        P("seq", "head", None),
        P("seq", "head", None),
        P("head", None),
    )
    out_specs = P("seq", "head")
    return jax.shard_map(
        on_device, mesh=mesh, in_specs=in_specs, out_specs=out_specs, check_vma=False
    )
```

profile of v0, /device:TPU:124, one launch (start us, length us, event | category | flops | bytes accessed | tf_op | source)
XLA Modules:
  0.0 145.5 jit_solution(4479707599341661802)
XLA Ops:
  0.0 1.6 %pack.1 = bf16[512,128]{1,0:T(8,128)(2,1)} custom-call(bf16[256,128]{1,0:T(8,128)(2,1)} %bitcast.30, bf16[256,128]{1,0:T(8,128)(2,1)} %bitcast.31), custom_call_target="tpu_custom_call" | custom-call | tf_op jit(solution)/shard_map/pack/pallas_call | solution.py:262
  1.6 1.6 %collective-permute-start = (bf16[512,128]{1,0:T(8,128)(2,1)}, bf16[512,128]{1,0:T(8,128)(2,1)S(1)}, u32[]{:S(2)}, u32[]{:S(2)}) collective-permute-start(bf16[512,128]{1,0:T(8,128)(2,1)} %pack.1), channel_id=1, source_target_pairs={{0,0},{1,224},{2,2},{3,226},{4,4},{5,228},{6,6},{7,230},{8,8},{9,2... | collective-permute-start | bytes 393224 | tf_op jit(solution)/shard_map/ppermute | solution.py:60
  3.1 0.0 collective-permute-done
  3.2 0.0 collective-permute-start.3
  3.2 4.6 %collective-permute-start.2 = (bf16[512,128]{1,0:T(8,128)(2,1)S(1)}, bf16[512,128]{1,0:T(8,128)(2,1)S(1)}, u32[]{:S(2)}, u32[]{:S(2)}) collective-permute-start(bf16[512,128]{1,0:T(8,128)(2,1)S(1)} %collective-permute-done), channel_id=1, source_target_pairs={{0,28},{1,5},{2,30},{3,7},{4,8},{5,1},{6,10},{7,3},{8,4},{9,13},{1... | collective-permute-start | bytes 393224 | tf_op jit(solution)/shard_map/ppermute | solution.py:60
  7.8 1.0 collective-permute-start.1
  8.8 1.1 copy.7
  9.9 0.4 collective-permute-done.3
  10.3 1.3 collective-permute-done.2
  11.6 1.1 collective-permute-done.1
  12.8 2.2 %collective-permute-start.5 = (bf16[2048,128]{1,0:T(8,128)(2,1)S(1)}, bf16[2048,128]{1,0:T(8,128)(2,1)S(1)}, u32[]{:S(2)}, u32[]{:S(2)}) collective-permute-start(bf16[2048,128]{1,0:T(8,128)(2,1)S(1)} %get-tuple-element.37.refs_0_), channel_id=1, source_target_pairs={{0,64},{1,193},{2,66},{3,195},{4,68},{5,197},{6,70},{7,199},{8,72}... | collective-permute-start | bytes 1572872 | tf_op jit(solution)/shard_map/ppermute | solution.py:60
  15.1 0.7 collective-permute-start.4
  15.8 0.1 collective-permute-start.6
  15.9 1.9 %collective-permute-start.7 = (bf16[1024,128]{1,0:T(8,128)(2,1)S(1)}, bf16[1024,128]{1,0:T(8,128)(2,1)S(1)}, u32[]{:S(2)}, u32[]{:S(2)}) collective-permute-start(bf16[1024,128]{1,0:T(8,128)(2,1)S(1)} %get-tuple-element.53), channel_id=1, source_target_pairs={{0,8},{1,25},{2,10},{3,27},{4,28},{5,13},{6,30},{7,15},{8,16},{9,1... | collective-permute-start | bytes 786440 | tf_op jit(solution)/shard_map/ppermute | solution.py:60
  17.8 1.1 collective-permute-start.10
  18.9 3.4 %collective-permute-done.6 = bf16[1024,128]{1,0:T(8,128)(2,1)S(1)} collective-permute-done((bf16[1024,128]{1,0:T(8,128)(2,1)S(1)}, bf16[1024,128]{1,0:T(8,128)(2,1)S(1)}, u32[]{:S(2)}, u32[]{:S(2)}) %collective-permute-start.6) | collective-permute-done | bytes 262176 | tf_op jit(solution)/shard_map/ppermute | solution.py:60
  22.2 2.9 %collective-permute-done.7 = bf16[1024,128]{1,0:T(8,128)(2,1)S(1)} collective-permute-done((bf16[1024,128]{1,0:T(8,128)(2,1)S(1)}, bf16[1024,128]{1,0:T(8,128)(2,1)S(1)}, u32[]{:S(2)}, u32[]{:S(2)}) %collective-permute-start.7) | collective-permute-done | bytes 262176 | tf_op jit(solution)/shard_map/ppermute | solution.py:60
  25.1 0.0 collective-permute-done.5.refs_1_
  25.1 0.0 collective-permute-done.4
  25.2 14.0 %collective-permute-start.8 = (bf16[2048,128]{1,0:T(8,128)(2,1)S(1)}, bf16[2048,128]{1,0:T(8,128)(2,1)S(1)}, u32[]{:S(2)}, u32[]{:S(2)}) collective-permute-start(bf16[2048,128]{1,0:T(8,128)(2,1)S(1)} %collective-permute-done.4), channel_id=1, source_target_pairs={{0,1},{1,0},{2,3},{3,2},{4,5},{5,4},{6,7},{7,6},{8,9},{9,8},{10,11... | collective-permute-start | bytes 1572872 | tf_op jit(solution)/shard_map/ppermute | solution.py:60
  39.1 0.1 stack.117.rows
  39.2 0.1 stack.113.info
  39.3 0.1 stack.126.zs
  39.4 0.1 collective-permute-start.12
  39.5 0.1 collective-permute-start.9
  39.6 3.1 %collective-permute-start.11 = (bf16[2048,128]{1,0:T(8,128)(2,1)S(1)}, bf16[2048,128]{1,0:T(8,128)(2,1)S(1)}, u32[]{:S(2)}, u32[]{:S(2)}) collective-permute-start(bf16[2048,128]{1,0:T(8,128)(2,1)S(1)} %collective-permute-done.5.refs_1_), channel_id=1, source_target_pairs={{0,192},{1,65},{2,194},{3,67},{4,196},{5,69},{6,198},{7,71},{8,200... | collective-permute-start | bytes 1572872 | tf_op jit(solution)/shard_map/ppermute | solution.py:60
  42.7 0.0 collective-permute-done.10.refs_2_
  42.7 0.0 collective-permute-done.8
  42.7 0.1 pad_maximum_fusion.q_ref
  42.8 0.0 slice-start
  42.9 9.3 %attend_0.1.refs_4_ = f32[2,144,2048]{2,1,0:T(8,128)S(1)} custom-call(s32[9]{0:T(128)S(1)} %stack.113.info, s32[8]{0:T(128)S(1)} %stack.117.rows, s32[32]{0:T(128)S(1)} %stack.126.zs, bf16[2,2048,128]{2,1,0:T(8,128)(2,1)S(1)} %pad_maximum_fusion.q_ref, bf16[2048,128]{1,0:T(8,128)(2,1)S(1)} %get-tuple-element.37.refs_0_, ...), custom_call_target="tpu_custom_call" | custom-call | flops 6442450944 | bytes 4194304 | tf_op jit(solution)/shard_map/attend_0/pallas_call | solution.py:176
  52.1 0.0 slice-start.1
  52.2 2.2 %collective-permute-done.9.refs_1_.refs_4_ = bf16[2048,128]{1,0:T(8,128)(2,1)S(1)} collective-permute-done((bf16[2048,128]{1,0:T(8,128)(2,1)S(1)}, bf16[2048,128]{1,0:T(8,128)(2,1)S(1)}, u32[]{:S(2)}, u32[]{:S(2)}) %collective-permute-start.9) | collective-permute-done | bytes 524320 | tf_op jit(solution)/shard_map/ppermute | solution.py:60
  54.4 3.2 %collective-permute-start.13 = (bf16[2048,128]{1,0:T(8,128)(2,1)S(1)}, bf16[2048,128]{1,0:T(8,128)(2,1)S(1)}, u32[]{:S(2)}, u32[]{:S(2)}) collective-permute-start(bf16[2048,128]{1,0:T(8,128)(2,1)S(1)} %collective-permute-done.9.refs_1_.refs_4_), channel_id=1, source_target_pairs={{0,192},{1,65},{2,194},{3,67},{4,196},{5,69},{6,198},{7,71},{8,200... | collective-permute-start | bytes 1572872 | tf_op jit(solution)/shard_map/ppermute | solution.py:60
  57.6 0.0 collective-permute-done.12.refs_3_.refs_6_
  57.6 2.7 %collective-permute-done.11.refs_2_.refs_5_ = bf16[2048,128]{1,0:T(8,128)(2,1)S(1)} collective-permute-done((bf16[2048,128]{1,0:T(8,128)(2,1)S(1)}, bf16[2048,128]{1,0:T(8,128)(2,1)S(1)}, u32[]{:S(2)}, u32[]{:S(2)}) %collective-permute-start.11) | collective-permute-done | bytes 524320 | tf_op jit(solution)/shard_map/ppermute | solution.py:60
  60.3 11.1 %attend_3.1.state = f32[2,144,2048]{2,1,0:T(8,128)S(1)} custom-call(s32[9]{0:T(128)S(1)} %stack.113.info, s32[8]{0:T(128)S(1)} %stack.117.rows, s32[32]{0:T(128)S(1)} %stack.126.zs, bf16[2,2048,128]{2,1,0:T(8,128)(2,1)S(1)} %pad_maximum_fusion.q_ref, ...), custom_call_target="tpu_custom_call", output_to_operand_aliasing={{}: (8, {})} | custom-call | flops 8589934592 | bytes 4194304 | tf_op jit(solution)/shard_map/attend_3/pallas_call | solution.py:176
  71.4 0.0 collective-permute-done.13.refs_7_
  71.4 37.4 %attend_last.1 = (f32[2,144,2048]{2,1,0:T(8,128)S(1)}, f32[144,2048]{1,0:T(8,128)S(1)}, f32[144,2048]{1,0:T(8,128)S(1)}) custom-call(s32[9]{0:T(128)S(1)} %stack.113.info, s32[8]{0:T(128)S(1)} %stack.117.rows, s32[32]{0:T(128)S(1)} %stack.126.zs, bf16[2,2048,128]{2,1,0:T(8,128)(2,1)S(1)} %pad_maximum_fusion.q_ref, ...), custom_call_target="tpu_custom_call", output_to_operand_aliasing={{0}: (4, {})} | custom-call | flops 2147483648 | bytes 4194304 | tf_op jit(solution)/shard_map/attend_last/pallas_call | solution.py:219
  108.8 0.3 collective-permute-start.14
  109.1 2.8 %collective-permute-done.14.b_ref = f32[144,2048]{1,0:T(8,128)S(1)} collective-permute-done((f32[144,2048]{1,0:T(8,128)S(1)}, f32[144,2048]{1,0:T(8,128)S(1)}, u32[]{:S(2)}, u32[]{:S(2)}) %collective-permute-start.14) | collective-permute-done | bytes 1179680 | tf_op jit(solution)/shard_map/ppermute | solution.py:60
  112.0 0.3 merge.1.home_ref
  112.2 0.7 collective-permute-start.15
  112.9 0.0 slice-done
  113.0 0.0 slice-done.1
  113.0 1.6 %load_8.1.w_ref = bf16[1024,2048]{1,0:T(8,128)(2,1)S(1)} custom-call(s32[9]{0:T(128)S(1)} %stack.113.info, bf16[1024,4096]{1,0:T(8,128)(2,1)S(1)} %bitcast.25), custom_call_target="tpu_custom_call" | custom-call | bytes 8388608 | tf_op jit(solution)/shard_map/load_8/pallas_call | solution.py:279
  114.6 0.0 collective-permute-done.15.away_ref
  114.6 1.8 %project.2 = (bf16[256,1024]{1,0:T(8,128)(2,1)S(1)}, f32[256,1024]{1,0:T(8,128)S(1)}) custom-call(s32[9]{0:T(128)S(1)} %stack.113.info, bf16[256,1024]{1,0:T(8,128)(2,1)S(1)} %merge.1.home_ref, bf16[256,1024]{1,0:T(8,128)(2,1)S(1)} %collective-permute-done.15.away_ref, bf16[1024,2048]{1,0:T(8,128)(2,1)S(1)} %load_8.1.w_ref), custom_call_target="tpu_custom_call" | custom-call | tf_op jit(solution)/shard_map/project/pallas_call | solution.py:306
  116.4 10.5 %collective-permute-start.16 = (bf16[256,1024]{1,0:T(8,128)(2,1)S(1)}, bf16[256,1024]{1,0:T(8,128)(2,1)S(1)}, u32[]{:S(2)}, u32[]{:S(2)}) collective-permute-start(bf16[256,1024]{1,0:T(8,128)(2,1)S(1)} %get-tuple-element.47), channel_id=1, source_target_pairs={{0,1},{1,0},{2,3},{3,2},{4,5},{5,4},{6,7},{7,6},{8,9},{9,8},{10,11... | collective-permute-start | bytes 1572872 | tf_op jit(solution)/shard_map/ppermute | solution.py:60
  127.0 1.5 %collective-permute-done.16 = bf16[256,1024]{1,0:T(8,128)(2,1)S(1)} collective-permute-done((bf16[256,1024]{1,0:T(8,128)(2,1)S(1)}, bf16[256,1024]{1,0:T(8,128)(2,1)S(1)}, u32[]{:S(2)}, u32[]{:S(2)}) %collective-permute-start.16) | collective-permute-done | bytes 524320 | tf_op jit(solution)/shard_map/ppermute | solution.py:60
  128.5 0.1 add_convert_fusion.1
  128.6 0.6 collective-permute-start.18
  129.2 1.6 %load_7.1.w_ref = bf16[1024,2048]{1,0:T(8,128)(2,1)S(1)} custom-call(s32[9]{0:T(128)S(1)} %stack.113.info, bf16[1024,4096]{1,0:T(8,128)(2,1)S(1)} %bitcast.25), custom_call_target="tpu_custom_call" | custom-call | bytes 8388608 | tf_op jit(solution)/shard_map/load_7/pallas_call | solution.py:279
  130.8 1.8 %project.3 = (bf16[256,1024]{1,0:T(8,128)(2,1)S(1)}, f32[256,1024]{1,0:T(8,128)S(1)}) custom-call(s32[9]{0:T(128)S(1)} %stack.113.info, bf16[256,1024]{1,0:T(8,128)(2,1)S(1)} %merge.1.home_ref, bf16[256,1024]{1,0:T(8,128)(2,1)S(1)} %collective-permute-done.15.away_ref, bf16[1024,2048]{1,0:T(8,128)(2,1)S(1)} %load_7.1.w_ref), custom_call_target="tpu_custom_call" | custom-call | tf_op jit(solution)/shard_map/project/pallas_call | solution.py:306
  132.7 0.2 collective-permute-start.17
  132.9 11.5 %collective-permute-done.18 = bf16[256,1024]{1,0:T(8,128)(2,1)S(1)} collective-permute-done((bf16[256,1024]{1,0:T(8,128)(2,1)S(1)}, bf16[256,1024]{1,0:T(8,128)(2,1)S(1)}, u32[]{:S(2)}, u32[]{:S(2)}) %collective-permute-start.18) | collective-permute-done | bytes 524320 | tf_op jit(solution)/shard_map/ppermute | solution.py:60
  144.4 0.0 collective-permute-done.17
  144.4 1.0 add_convert_fusion
  (7 shorter events, 0.2 us)
Async XLA Ops:
  1.6 1.6 %collective-permute-start = (bf16[512,128]{1,0:T(8,128)(2,1)}, bf16[512,128]{1,0:T(8,128)(2,1)S(1)}, u32[]{:S(2)}, u32[]{:S(2)}) collective-permute-start(bf16[512,128]{1,0:T(8,128)(2,1)} %pack.1), channel_id=1, source_target_pairs={{0,0},{1,224},{2,2},{3,226},{4,4},{5,228},{6,6},{7,230},{8,8},{9,2... | collective-permute-start | bytes 393224 | tf_op jit(solution)/shard_map/ppermute | solution.py:60
  3.2 7.2 %collective-permute-start.3 = (bf16[512,128]{1,0:T(8,128)(2,1)S(1)}, bf16[512,128]{1,0:T(8,128)(2,1)S(1)}, u32[]{:S(2)}, u32[]{:S(2)}) collective-permute-start(bf16[512,128]{1,0:T(8,128)(2,1)S(1)} %collective-permute-done), channel_id=1, source_target_pairs={{0,8},{1,25},{2,10},{3,27},{4,28},{5,13},{6,30},{7,15},{8,16},{9,1... | collective-permute-start | bytes 393224 | tf_op jit(solution)/shard_map/ppermute | solution.py:60
  3.2 8.5 %collective-permute-start.2 = (bf16[512,128]{1,0:T(8,128)(2,1)S(1)}, bf16[512,128]{1,0:T(8,128)(2,1)S(1)}, u32[]{:S(2)}, u32[]{:S(2)}) collective-permute-start(bf16[512,128]{1,0:T(8,128)(2,1)S(1)} %collective-permute-done), channel_id=1, source_target_pairs={{0,28},{1,5},{2,30},{3,7},{4,8},{5,1},{6,10},{7,3},{8,4},{9,13},{1... | collective-permute-start | bytes 393224 | tf_op jit(solution)/shard_map/ppermute | solution.py:60
  7.8 5.0 %collective-permute-start.1 = (bf16[512,128]{1,0:T(8,128)(2,1)S(1)}, bf16[512,128]{1,0:T(8,128)(2,1)S(1)}, u32[]{:S(2)}, u32[]{:S(2)}) collective-permute-start(bf16[512,128]{1,0:T(8,128)(2,1)S(1)} %collective-permute-done), channel_id=1, source_target_pairs={{0,4},{1,29},{2,6},{3,31},{4,0},{5,9},{6,2},{7,11},{8,12},{9,5},{1... | collective-permute-start | bytes 393224 | tf_op jit(solution)/shard_map/ppermute | solution.py:60
  12.8 12.3 %collective-permute-start.5 = (bf16[2048,128]{1,0:T(8,128)(2,1)S(1)}, bf16[2048,128]{1,0:T(8,128)(2,1)S(1)}, u32[]{:S(2)}, u32[]{:S(2)}) collective-permute-start(bf16[2048,128]{1,0:T(8,128)(2,1)S(1)} %get-tuple-element.37.refs_0_), channel_id=1, source_target_pairs={{0,64},{1,193},{2,66},{3,195},{4,68},{5,197},{6,70},{7,199},{8,72}... | collective-permute-start | bytes 1572872 | tf_op jit(solution)/shard_map/ppermute | solution.py:60
  15.1 10.1 %collective-permute-start.4 = (bf16[2048,128]{1,0:T(8,128)(2,1)S(1)}, bf16[2048,128]{1,0:T(8,128)(2,1)S(1)}, u32[]{:S(2)}, u32[]{:S(2)}) collective-permute-start(bf16[2048,128]{1,0:T(8,128)(2,1)S(1)} %bitcast.27), channel_id=1, source_target_pairs={{0,0},{1,224},{2,2},{3,226},{4,4},{5,228},{6,6},{7,230},{8,8},{9,2... | collective-permute-start | bytes 1572872 | tf_op jit(solution)/shard_map/ppermute | solution.py:60
  15.8 6.5 %collective-permute-start.6 = (bf16[1024,128]{1,0:T(8,128)(2,1)S(1)}, bf16[1024,128]{1,0:T(8,128)(2,1)S(1)}, u32[]{:S(2)}, u32[]{:S(2)}) collective-permute-start(bf16[1024,128]{1,0:T(8,128)(2,1)S(1)} %get-tuple-element.53), channel_id=1, source_target_pairs={{0,4},{1,29},{2,6},{3,31},{4,0},{5,9},{6,2},{7,11},{8,12},{9,5},{1... | collective-permute-start | bytes 786440 | tf_op jit(solution)/shard_map/ppermute | solution.py:60
  15.9 9.2 %collective-permute-start.7 = (bf16[1024,128]{1,0:T(8,128)(2,1)S(1)}, bf16[1024,128]{1,0:T(8,128)(2,1)S(1)}, u32[]{:S(2)}, u32[]{:S(2)}) collective-permute-start(bf16[1024,128]{1,0:T(8,128)(2,1)S(1)} %get-tuple-element.53), channel_id=1, source_target_pairs={{0,8},{1,25},{2,10},{3,27},{4,28},{5,13},{6,30},{7,15},{8,16},{9,1... | collective-permute-start | bytes 786440 | tf_op jit(solution)/shard_map/ppermute | solution.py:60
  17.8 24.9 %collective-permute-start.10 = (bf16[2048,128]{1,0:T(8,128)(2,1)S(1)}, bf16[2048,128]{1,0:T(8,128)(2,1)S(1)}, u32[]{:S(2)}, u32[]{:S(2)}) collective-permute-start(bf16[2048,128]{1,0:T(8,128)(2,1)S(1)} %get-tuple-element.37.refs_0_), channel_id=1, source_target_pairs={{0,192},{1,65},{2,194},{3,67},{4,196},{5,69},{6,198},{7,71},{8,200... | collective-permute-start | bytes 1572872 | tf_op jit(solution)/shard_map/ppermute | solution.py:60
  25.2 17.6 %collective-permute-start.8 = (bf16[2048,128]{1,0:T(8,128)(2,1)S(1)}, bf16[2048,128]{1,0:T(8,128)(2,1)S(1)}, u32[]{:S(2)}, u32[]{:S(2)}) collective-permute-start(bf16[2048,128]{1,0:T(8,128)(2,1)S(1)} %collective-permute-done.4), channel_id=1, source_target_pairs={{0,1},{1,0},{2,3},{3,2},{4,5},{5,4},{6,7},{7,6},{8,9},{9,8},{10,11... | collective-permute-start | bytes 1572872 | tf_op jit(solution)/shard_map/ppermute | solution.py:60
  39.4 18.2 %collective-permute-start.12 = (bf16[2048,128]{1,0:T(8,128)(2,1)S(1)}, bf16[2048,128]{1,0:T(8,128)(2,1)S(1)}, u32[]{:S(2)}, u32[]{:S(2)}) collective-permute-start(bf16[2048,128]{1,0:T(8,128)(2,1)S(1)} %constant_dynamic-update-slice_fusion.6.refs_0_.refs_3_), channel_id=1, source_target_pairs={{0,192},{1,65},{2,194},{3,67},{4,196},{5,69},{6,198},{7,71},{8,200... | collective-permute-start | bytes 1572872 | tf_op jit(solution)/shard_map/ppermute | solution.py:60
  39.5 14.9 %collective-permute-start.9 = (bf16[2048,128]{1,0:T(8,128)(2,1)S(1)}, bf16[2048,128]{1,0:T(8,128)(2,1)S(1)}, u32[]{:S(2)}, u32[]{:S(2)}) collective-permute-start(bf16[2048,128]{1,0:T(8,128)(2,1)S(1)} %constant_dynamic-update-slice_fusion.6.refs_0_.refs_3_), channel_id=1, source_target_pairs={{0,64},{1,193},{2,66},{3,195},{4,68},{5,197},{6,70},{7,199},{8,72}... | collective-permute-start | bytes 1572872 | tf_op jit(solution)/shard_map/ppermute | solution.py:60
  39.6 20.6 %collective-permute-start.11 = (bf16[2048,128]{1,0:T(8,128)(2,1)S(1)}, bf16[2048,128]{1,0:T(8,128)(2,1)S(1)}, u32[]{:S(2)}, u32[]{:S(2)}) collective-permute-start(bf16[2048,128]{1,0:T(8,128)(2,1)S(1)} %collective-permute-done.5.refs_1_), channel_id=1, source_target_pairs={{0,192},{1,65},{2,194},{3,67},{4,196},{5,69},{6,198},{7,71},{8,200... | collective-permute-start | bytes 1572872 | tf_op jit(solution)/shard_map/ppermute | solution.py:60
  42.8 70.1 %slice-start = ((s8[8388608]{0:T(1024)(128)(4,1)}), s8[4194304]{0:T(1024)(128)(4,1)S(1)}, s32[]{:S(2)}) async-start(s8[8388608]{0:T(1024)(128)(4,1)} %bitcast.24), calls=%async_computation | async-start | bytes 8388608
  52.1 60.8 %slice-start.1 = ((s8[8388608]{0:T(1024)(128)(4,1)}), s8[4194304]{0:T(1024)(128)(4,1)S(1)}, s32[]{:S(2)}) async-start(s8[8388608]{0:T(1024)(128)(4,1)} %bitcast.24), calls=%async_computation.1 | async-start | bytes 8388608
  54.4 17.0 %collective-permute-start.13 = (bf16[2048,128]{1,0:T(8,128)(2,1)S(1)}, bf16[2048,128]{1,0:T(8,128)(2,1)S(1)}, u32[]{:S(2)}, u32[]{:S(2)}) collective-permute-start(bf16[2048,128]{1,0:T(8,128)(2,1)S(1)} %collective-permute-done.9.refs_1_.refs_4_), channel_id=1, source_target_pairs={{0,192},{1,65},{2,194},{3,67},{4,196},{5,69},{6,198},{7,71},{8,200... | collective-permute-start | bytes 1572872 | tf_op jit(solution)/shard_map/ppermute | solution.py:60
  108.8 3.2 %collective-permute-start.14 = (f32[144,2048]{1,0:T(8,128)S(1)}, f32[144,2048]{1,0:T(8,128)S(1)}, u32[]{:S(2)}, u32[]{:S(2)}) collective-permute-start(f32[144,2048]{1,0:T(8,128)S(1)} %get-tuple-element.43), channel_id=1, source_target_pairs={{0,1},{1,0},{2,3},{3,2},{4,5},{5,4},{6,7},{7,6},{8,9},{9,8},{10,11... | collective-permute-start | bytes 3538952 | tf_op jit(solution)/shard_map/ppermute | solution.py:60
  112.2 2.3 %collective-permute-start.15 = (bf16[256,1024]{1,0:T(8,128)(2,1)S(1)}, bf16[256,1024]{1,0:T(8,128)(2,1)S(1)}, u32[]{:S(2)}, u32[]{:S(2)}) collective-permute-start(bf16[256,1024]{1,0:T(8,128)(2,1)S(1)} %merge.1.home_ref), channel_id=1, source_target_pairs={{1,224},{3,226},{5,228},{7,230},{9,232},{11,234},{13,236},{15,238}... | collective-permute-start | bytes 1572872 | tf_op jit(solution)/shard_map/ppermute | solution.py:60
  116.4 12.1 %collective-permute-start.16 = (bf16[256,1024]{1,0:T(8,128)(2,1)S(1)}, bf16[256,1024]{1,0:T(8,128)(2,1)S(1)}, u32[]{:S(2)}, u32[]{:S(2)}) collective-permute-start(bf16[256,1024]{1,0:T(8,128)(2,1)S(1)} %get-tuple-element.47), channel_id=1, source_target_pairs={{0,1},{1,0},{2,3},{3,2},{4,5},{5,4},{6,7},{7,6},{8,9},{9,8},{10,11... | collective-permute-start | bytes 1572872 | tf_op jit(solution)/shard_map/ppermute | solution.py:60
  128.6 15.8 %collective-permute-start.18 = (bf16[256,1024]{1,0:T(8,128)(2,1)S(1)}, bf16[256,1024]{1,0:T(8,128)(2,1)S(1)}, u32[]{:S(2)}, u32[]{:S(2)}) collective-permute-start(bf16[256,1024]{1,0:T(8,128)(2,1)S(1)} %add_convert_fusion.1), channel_id=1, source_target_pairs={{0,2},{1,3},{2,0},{3,1},{4,6},{5,7},{6,4},{7,5},{8,10},{9,11},{10,... | collective-permute-start | bytes 1572872 | tf_op jit(solution)/shard_map/ppermute | solution.py:60
  132.7 11.8 %collective-permute-start.17 = (bf16[256,1024]{1,0:T(8,128)(2,1)S(1)}, bf16[256,1024]{1,0:T(8,128)(2,1)S(1)}, u32[]{:S(2)}, u32[]{:S(2)}) collective-permute-start(bf16[256,1024]{1,0:T(8,128)(2,1)S(1)} %get-tuple-element.51), channel_id=1, source_target_pairs={{0,1},{1,0},{2,3},{3,2},{4,5},{5,4},{6,7},{7,6},{8,9},{9,8},{10,11... | collective-permute-start | bytes 1572872 | tf_op jit(solution)/shard_map/ppermute | solution.py:60
where the time goes:
time: 148 us; the launch traced here: 145 us
  Pallas kernels  66.5 us (45%)
  starting transfers between devices  46 us (31%)
  waiting for transfers between devices  29.9 us (20%)
  local copies, waits for them, and re-layouts  1.57 us (1%)
    ppermute x19, starting transfers between devices, send(): return lax.ppermute(value, AXES, perm)  46 us
    pallas_call x1, Pallas kernels, attend_last(): pl.pallas_call(functools.partial(last_kernel, len(pieces)), out_shape=(ST...  37.4 us
    ppermute x19, waiting for transfers between devices, send(): return lax.ppermute(value, AXES, perm)  29.9 us
    pallas_call x2, Pallas kernels, attend_pieces(): pl.pallas_call(functools.partial(piece_kernel, first, n_tiles, state is n...  20.4 us
    pallas_call x2, Pallas kernels, project(): pl.pallas_call(project_kernel, out_shape=(jax.ShapeDtypeStruct((TOK, SLIC...  3.68 us
    pallas_call x2, Pallas kernels, load_columns(): pl.pallas_call(functools.partial(load_kernel, first), out_shape=jax.Shape...  3.18 us
  transfers between devices with their start and end apart: 19, of which 10 were waited for; matrix products, arithmetic and copies ran while one was open for 1% of the time, Pallas kernels for 17%

commit v1 on v0

--- a/solution.py
+++ b/solution.py
@@ -46,6 +46,7 @@
 
 
 SWAP = perm_of(lambda X, y, x, z, c: (X, y, x, z, c) if c == x else (X, 3 - y, 1 - x, z, 1 - c))
+KV_SWAP = perm_of(lambda X, y, x, z, c: (X, y, x, z, c) if c == x else (X, y, 1 - x, z, 1 - c))
 SWAP_BACK = [pair for pair in SWAP if pair[0] != pair[1]]
 CORE = perm_of(lambda X, y, x, z, c: (X, y, x, z, 1 - c))
 XHI = perm_of(lambda X, y, x, z, c: (1 - X, y, x, z, c))
@@ -160,6 +161,7 @@
 SMEM = pl.BlockSpec(memory_space=pltpu.SMEM)
 STATE = jax.ShapeDtypeStruct((2, DEEP, ROWS), jnp.float32)
 PART = jax.ShapeDtypeStruct((DEEP, ROWS), jnp.float32)
+GIVEN = jax.ShapeDtypeStruct((DEEP, ROWS), jnp.bfloat16)
 
 
 def cost(n_tiles):
@@ -186,21 +188,29 @@
     )(info, rows, zs, q, *pieces, *extra)
 
 
+def in_parts(row, n):
+    parts = []
+    for _ in range(n):
+        parts.append(row.astype(jnp.bfloat16).astype(jnp.float32))
+        row = row - parts[-1]
+    return parts
+
+
 def last_kernel(n_pieces, info, rows, zs, q_ref, state, *refs):
     pieces = refs[:n_pieces]
     acc, keep_ref, give_ref, k_ref, v_ref, top = refs[n_pieces:]
     last = n_pieces - 1
     place(pieces[last], k_ref, v_ref, last)
     fast_blocks(info, rows, zs, last, 1, last, q_ref, k_ref, v_ref, acc)
-    for block, out_ref in enumerate((keep_ref, give_ref)):
+    for block in range(2):
         total = acc[block, HD : HD + 8, :]
         bad = jnp.logical_not(jnp.logical_and(total >= LOW, total <= HIGH))
         n_bad = jnp.sum(jnp.max(bad.astype(jnp.float32), axis=0, keepdims=True))
         some = jnp.logical_or(info[block] > 0, info[2 + block] >= 0)
-        out_ref[HD + 8 :, :] = jnp.full((8, ROWS), jnp.where(some, 0.0, NEG), jnp.float32)
+        top[...] = jnp.full((8, ROWS), jnp.where(some, 0.0, NEG), jnp.float32)
 
         @pl.when(jnp.logical_and(some, n_bad > 0.0))
-        def _(block=block, out_ref=out_ref):
+        def _(block=block):
             acc[block] = jnp.zeros((DEEP, ROWS), jnp.float32)
             top[...] = jnp.full((8, ROWS), NEG, jnp.float32)
             for t, piece in enumerate(pieces[:last]):
@@ -210,15 +220,24 @@
                 slow_tile(q_ref, k_ref, v_ref, acc, top, block, t, aheads)
 
             tiles(run, info, rows, zs, 0, n_pieces, 0, block, False)
-            out_ref[HD + 8 :, :] = top[...]
-
-        out_ref[: HD + 8, :] = acc[block, : HD + 8, :]
+
+        if block == 0:
+            keep_ref[: HD + 8, :] = acc[block, : HD + 8, :]
+            keep_ref[HD + 8 :, :] = top[...]
+        else:
+            give_ref[:HD, :] = acc[block, :HD, :].astype(jnp.bfloat16)
+            parts = in_parts(acc[block, HD : HD + 1, :], 2) + in_parts(top[:1, :], 3)
+            row = lax.broadcasted_iota(jnp.int32, (DEEP - HD, ROWS), 0)
+            ends = jnp.zeros((DEEP - HD, ROWS), jnp.float32)
+            for i, part in enumerate(parts):
+                ends = jnp.where(row == i, part, ends)
+            give_ref[HD:, :] = ends.astype(jnp.bfloat16)
 
 
 def attend_last(info, rows, zs, q, state, pieces):
     return pl.pallas_call(
         functools.partial(last_kernel, len(pieces)),
-        out_shape=(STATE, PART, PART),
+        out_shape=(STATE, PART, GIVEN),
         in_specs=[SMEM, SMEM, SMEM] + [VMEM] * (2 + len(pieces)),
         out_specs=(VMEM, VMEM, VMEM),
         scratch_shapes=tile_scratch(len(pieces)) + [pltpu.VMEM((8, ROWS), jnp.float32)],
@@ -230,14 +249,17 @@
 
 
 def merge_kernel(a_ref, b_ref, out_ref):
-    sums, tops = slice(HD, HD + 1), slice(HD + 8, HD + 9)
-    top = jnp.maximum(a_ref[tops, :], b_ref[tops, :])
-    fa, fb = jnp.exp2(a_ref[tops, :] - top), jnp.exp2(b_ref[tops, :] - top)
-    total = a_ref[sums, :] * fa + b_ref[sums, :] * fb
+    a_sum, a_top = a_ref[HD : HD + 1, :], a_ref[HD + 8 : HD + 9, :]
+    ends = b_ref[HD:, :].astype(jnp.float32)
+    b_sum = ends[0:1] + ends[1:2]
+    b_top = ends[2:3] + ends[3:4] + ends[4:5]
+    top = jnp.maximum(a_top, b_top)
+    fa, fb = jnp.exp2(a_top - top), jnp.exp2(b_top - top)
+    total = a_sum * fa + b_sum * fb
     fa, fb = fa / total, fb / total
     for h in range(HEADS):
         at = slice(h * TOK, (h + 1) * TOK)
-        value = a_ref[:HD, at] * fa[:, at] + b_ref[:HD, at] * fb[:, at]
+        value = a_ref[:HD, at] * fa[:, at] + b_ref[:HD, at].astype(jnp.float32) * fb[:, at]
         out_ref[:, h * HD : (h + 1) * HD] = value.T.astype(jnp.bfloat16)
 
 
@@ -326,7 +348,7 @@
 
     k = key_states.reshape(TOK, HD)
     v = value_vectors_all.reshape(TOK, HD)
-    kv = send(pack(k, v), SWAP)
+    kv = send(pack(k, v), KV_SWAP)
     q = queries.transpose(1, 0, 2).reshape(ROWS, HD)
 
     sz, sy = sign_of(z, c), sign_of(y, c)
@@ -338,30 +360,27 @@
     a_near, a_far = send(a, Y_NEAR), send(a, Y_FAR)
     b = jnp.concatenate([send(side, Z_NEAR), send(side, Z_SKIP)], axis=0)
     b_near, b_far = send(b, Y_NEAR), send(b, Y_FAR)
-    a_near, b = lax.optimization_barrier((a_near, b))
+    a_near, a_far, b = lax.optimization_barrier((a_near, a_far, b))
     a_last = send(a_near, Y_FAR)
     q_own, b = lax.optimization_barrier((q_own, b))
     q_other = send(q_own, CORE)
 
-    def block_row(chip_y):
-        return jnp.where(diagonal, chip_y % NY, NY - 1 - chip_y % NY)
-
-    own_row = block_row(y)
+    own_row = jnp.where(diagonal, y, NY - 1 - y)
     other_rows = NY - 1 - own_row + jnp.where(c == 0, 1, 0)
     info = jnp.stack([own_row, other_rows, own_row, jnp.int32(-1), z, diagonal, c, 2 * X, 2 - 2 * X]).astype(jnp.int32)
-    near, far, last = block_row(y + sy), block_row(y - sy), block_row(y - 2 * sy)
-    rows = jnp.stack([own_row, near, far, own_row, near, last, far, last]).astype(jnp.int32)
+    near, far, last = y + sy, y - sy, y - 2 * sy
+    rows = jnp.stack([w % NY for w in (y, near, far, y, last, near, far, last)]).astype(jnp.int32)
     z_a = [z, z + sz, z - sz, z - 2 * sz]
     z_b = [z + 2 * sz, z + 3 * sz, z - 3 * sz, z - 4 * sz]
-    zs = jnp.stack([w % NZ for w in z_a * 3 + z_b * 2 + z_a + z_b * 2]).astype(jnp.int32)
+    zs = jnp.stack([w % NZ for w in z_a * 3 + z_b + z_a + z_b * 3]).astype(jnp.int32)
     q = jnp.stack([q_own, q_other])
 
-    early = [a, a_near, a_far]
-    state = attend_pieces(info, rows, zs, q, lax.optimization_barrier((early, b))[0], 0)
+    early = [a, a_near, a_far, b]
+    state = attend_pieces(info, rows, zs, q, early, 0)
     b_near, state = lax.optimization_barrier((b_near, state))
     b_last = send(b_near, Y_FAR)
-    middle = [b, b_near, a_last, b_far]
-    state = attend_pieces(info, rows, zs, q, middle, 3, state)
+    middle = [a_last, b_near, b_far]
+    state = attend_pieces(info, rows, zs, q, middle, 4, state)
     pieces = early + middle + [b_last]
     keep, give = attend_last(info, rows, zs, q, state, pieces)
     home = merge(keep, send(give, CORE))

time: 148 us -> 146 us (0.986)
  the two profiles are of different devices: /device:TPU:124 before, /device:TPU:196 now
where the time goes in v1:
time: 146 us; the launch traced here: 145 us
  Pallas kernels  76.2 us (52%)
  starting transfers between devices  36.8 us (25%)
  waiting for transfers between devices  29.3 us (20%)
  local copies, waits for them, and re-layouts  1.57 us (1%)
    pallas_call x1, Pallas kernels, attend_last(): pl.pallas_call(functools.partial(last_kernel, len(pieces)), out_shape=(ST...  47 us
    ppermute x19, starting transfers between devices, send(): return lax.ppermute(value, AXES, perm)  36.8 us
    ppermute x19, waiting for transfers between devices, send(): return lax.ppermute(value, AXES, perm)  29.3 us
    pallas_call x2, Pallas kernels, attend_pieces(): pl.pallas_call(functools.partial(piece_kernel, first, n_tiles, state is n...  20.4 us
    pallas_call x2, Pallas kernels, project(): pl.pallas_call(project_kernel, out_shape=(jax.ShapeDtypeStruct((TOK, SLIC...  3.68 us
    pallas_call x2, Pallas kernels, load_columns(): pl.pallas_call(functools.partial(load_kernel, first), out_shape=jax.Shape...  3.18 us
  transfers between devices with their start and end apart: 19, of which 11 were waited for; matrix products, arithmetic and copies ran while one was open for 1% of the time, Pallas kernels for 17%

profile of v1, /device:TPU:196, one launch (start us, length us, event | category | flops | bytes accessed | tf_op | source)
XLA Modules:
  0.0 145.3 jit_solution(13831557094006005300)
XLA Ops:
  0.0 1.6 %pack.1 = bf16[512,128]{1,0:T(8,128)(2,1)} custom-call(bf16[256,128]{1,0:T(8,128)(2,1)} %bitcast.31, bf16[256,128]{1,0:T(8,128)(2,1)} %bitcast.32), custom_call_target="tpu_custom_call" | custom-call | tf_op jit(solution)/shard_map/pack/pallas_call | solution.py:284
  1.6 1.6 %collective-permute-start = (bf16[512,128]{1,0:T(8,128)(2,1)}, bf16[512,128]{1,0:T(8,128)(2,1)S(1)}, u32[]{:S(2)}, u32[]{:S(2)}) collective-permute-start(bf16[512,128]{1,0:T(8,128)(2,1)} %pack.1), channel_id=1, source_target_pairs={{0,0},{1,32},{2,2},{3,34},{4,4},{5,36},{6,6},{7,38},{8,8},{9,40},{... | collective-permute-start | bytes 393224 | tf_op jit(solution)/shard_map/ppermute | solution.py:61
  3.1 0.0 collective-permute-done
  3.2 0.0 collective-permute-start.3
  3.2 1.6 %collective-permute-start.2 = (bf16[512,128]{1,0:T(8,128)(2,1)S(1)}, bf16[512,128]{1,0:T(8,128)(2,1)S(1)}, u32[]{:S(2)}, u32[]{:S(2)}) collective-permute-start(bf16[512,128]{1,0:T(8,128)(2,1)S(1)} %collective-permute-done), channel_id=1, source_target_pairs={{0,28},{1,5},{2,30},{3,7},{4,8},{5,1},{6,10},{7,3},{8,4},{9,13},{1... | collective-permute-start | bytes 393224 | tf_op jit(solution)/shard_map/ppermute | solution.py:61
  4.7 0.9 collective-permute-start.1
  5.6 1.1 copy.7
  6.8 2.4 %collective-permute-done.3 = bf16[512,128]{1,0:T(8,128)(2,1)S(1)} collective-permute-done((bf16[512,128]{1,0:T(8,128)(2,1)S(1)}, bf16[512,128]{1,0:T(8,128)(2,1)S(1)}, u32[]{:S(2)}, u32[]{:S(2)}) %collective-permute-start.3) | collective-permute-done | bytes 131104 | tf_op jit(solution)/shard_map/ppermute | solution.py:61
  9.1 0.4 collective-permute-done.2
  9.5 0.5 collective-permute-done.1
  10.1 3.1 %collective-permute-start.6 = (bf16[2048,128]{1,0:T(8,128)(2,1)S(1)}, bf16[2048,128]{1,0:T(8,128)(2,1)S(1)}, u32[]{:S(2)}, u32[]{:S(2)}) collective-permute-start(bf16[2048,128]{1,0:T(8,128)(2,1)S(1)} %get-tuple-element.50.refs_0_), channel_id=1, source_target_pairs={{0,192},{1,65},{2,194},{3,67},{4,196},{5,69},{6,198},{7,71},{8,200... | collective-permute-start | bytes 1572872 | tf_op jit(solution)/shard_map/ppermute | solution.py:61
  13.2 0.1 collective-permute-start.5
  13.4 0.7 collective-permute-start.4
  14.1 2.9 %collective-permute-start.7 = (bf16[1024,128]{1,0:T(8,128)(2,1)S(1)}, bf16[1024,128]{1,0:T(8,128)(2,1)S(1)}, u32[]{:S(2)}, u32[]{:S(2)}) collective-permute-start(bf16[1024,128]{1,0:T(8,128)(2,1)S(1)} %get-tuple-element.49), channel_id=1, source_target_pairs={{0,4},{1,29},{2,6},{3,31},{4,0},{5,9},{6,2},{7,11},{8,12},{9,5},{1... | collective-permute-start | bytes 786440 | tf_op jit(solution)/shard_map/ppermute | solution.py:61
  16.9 3.1 %collective-permute-start.8 = (bf16[1024,128]{1,0:T(8,128)(2,1)S(1)}, bf16[1024,128]{1,0:T(8,128)(2,1)S(1)}, u32[]{:S(2)}, u32[]{:S(2)}) collective-permute-start(bf16[1024,128]{1,0:T(8,128)(2,1)S(1)} %get-tuple-element.49), channel_id=1, source_target_pairs={{0,8},{1,25},{2,10},{3,27},{4,28},{5,13},{6,30},{7,15},{8,16},{9,1... | collective-permute-start | bytes 786440 | tf_op jit(solution)/shard_map/ppermute | solution.py:61
  20.0 1.3 collective-permute-done.7
  21.3 3.1 %collective-permute-done.8 = bf16[1024,128]{1,0:T(8,128)(2,1)S(1)} collective-permute-done((bf16[1024,128]{1,0:T(8,128)(2,1)S(1)}, bf16[1024,128]{1,0:T(8,128)(2,1)S(1)}, u32[]{:S(2)}, u32[]{:S(2)}) %collective-permute-start.8) | collective-permute-done | bytes 262176 | tf_op jit(solution)/shard_map/ppermute | solution.py:61
  24.4 0.0 collective-permute-done.6.refs_2_
  24.4 3.2 %collective-permute-done.5.refs_1_ = bf16[2048,128]{1,0:T(8,128)(2,1)S(1)} collective-permute-done((bf16[2048,128]{1,0:T(8,128)(2,1)S(1)}, bf16[2048,128]{1,0:T(8,128)(2,1)S(1)}, u32[]{:S(2)}, u32[]{:S(2)}) %collective-permute-start.5) | collective-permute-done | bytes 524320 | tf_op jit(solution)/shard_map/ppermute | solution.py:61
  27.7 0.0 collective-permute-done.4
  27.7 6.4 %collective-permute-start.9 = (bf16[2048,128]{1,0:T(8,128)(2,1)S(1)}, bf16[2048,128]{1,0:T(8,128)(2,1)S(1)}, u32[]{:S(2)}, u32[]{:S(2)}) collective-permute-start(bf16[2048,128]{1,0:T(8,128)(2,1)S(1)} %collective-permute-done.4), channel_id=1, source_target_pairs={{0,1},{1,0},{2,3},{3,2},{4,5},{5,4},{6,7},{7,6},{8,9},{9,8},{10,11... | collective-permute-start | bytes 1572872 | tf_op jit(solution)/shard_map/ppermute | solution.py:61
  34.0 0.1 stack.120.rows
  34.1 0.1 stack.129.zs
  34.2 0.1 stack.115.info
  34.3 2.6 %collective-permute-start.12 = (bf16[2048,128]{1,0:T(8,128)(2,1)S(1)}, bf16[2048,128]{1,0:T(8,128)(2,1)S(1)}, u32[]{:S(2)}, u32[]{:S(2)}) collective-permute-start(bf16[2048,128]{1,0:T(8,128)(2,1)S(1)} %constant_dynamic-update-slice_fusion.6.refs_3_), channel_id=1, source_target_pairs={{0,192},{1,65},{2,194},{3,67},{4,196},{5,69},{6,198},{7,71},{8,200... | collective-permute-start | bytes 1572872 | tf_op jit(solution)/shard_map/ppermute | solution.py:61
  36.9 0.4 collective-permute-start.11
  37.3 0.7 collective-permute-start.10
  38.0 0.0 collective-permute-done.9
  38.0 0.1 pad_maximum_fusion.q_ref
  38.1 0.0 slice-start
  38.1 13.8 %attend_0.1.refs_3_ = f32[2,144,2048]{2,1,0:T(8,128)S(1)} custom-call(s32[9]{0:T(128)S(1)} %stack.115.info, s32[8]{0:T(128)S(1)} %stack.120.rows, s32[32]{0:T(128)S(1)} %stack.129.zs, bf16[2,2048,128]{2,1,0:T(8,128)(2,1)S(1)} %pad_maximum_fusion.q_ref, bf16[2048,128]{1,0:T(8,128)(2,1)S(1)} %get-tuple-element.50.refs_0_, ...), custom_call_target="tpu_custom_call" | custom-call | flops 8589934592 | bytes 4194304 | tf_op jit(solution)/shard_map/attend_0/pallas_call | solution.py:178
  52.0 0.0 slice-start.1
  52.0 0.0 collective-permute-done.11.refs_1_.refs_5_
  52.0 0.9 collective-permute-start.13
  52.9 0.0 collective-permute-done.12.refs_2_.refs_6_
  52.9 2.8 %collective-permute-done.10.refs_0_.refs_4_ = bf16[2048,128]{1,0:T(8,128)(2,1)S(1)} collective-permute-done((bf16[2048,128]{1,0:T(8,128)(2,1)S(1)}, bf16[2048,128]{1,0:T(8,128)(2,1)S(1)}, u32[]{:S(2)}, u32[]{:S(2)}) %collective-permute-start.10) | collective-permute-done | bytes 524320 | tf_op jit(solution)/shard_map/ppermute | solution.py:61
  55.7 6.6 %attend_4.1.state = f32[2,144,2048]{2,1,0:T(8,128)S(1)} custom-call(s32[9]{0:T(128)S(1)} %stack.115.info, s32[8]{0:T(128)S(1)} %stack.120.rows, s32[32]{0:T(128)S(1)} %stack.129.zs, bf16[2,2048,128]{2,1,0:T(8,128)(2,1)S(1)} %pad_maximum_fusion.q_ref, bf16[2048,128]{1,0:T(8,128)(2,1)S(1)} %collective-permute-done.10.refs_0_.refs_4_, ...), custom_call_target="tpu_custom_call", output_to_operand_aliasing={{}: (7, {})} | custom-call | flops 6442450944 | bytes 4194304 | tf_op jit(solution)/shard_map/attend_4/pallas_call | solution.py:178
  62.3 0.4 collective-permute-done.13.refs_7_
  62.7 47.0 %attend_last.1 = (f32[2,144,2048]{2,1,0:T(8,128)S(1)}, f32[144,2048]{1,0:T(8,128)S(1)}, bf16[144,2048]{1,0:T(8,128)(2,1)S(1)}) custom-call(s32[9]{0:T(128)S(1)} %stack.115.info, s32[8]{0:T(128)S(1)} %stack.120.rows, s32[32]{0:T(128)S(1)} %stack.129.zs, bf16[2,2048,128]{2,1,0:T(8,128)(2,1)S(1)} %pad_maximum_fusion.q_ref, ...), custom_call_target="tpu_custom_call", output_to_operand_aliasing={{0}: (4, {})} | custom-call | flops 2147483648 | bytes 4194304 | tf_op jit(solution)/shard_map/attend_last/pallas_call | solution.py:238
  109.7 0.1 collective-permute-start.14
  109.8 2.0 %collective-permute-done.14.b_ref = bf16[144,2048]{1,0:T(8,128)(2,1)S(1)} collective-permute-done((bf16[144,2048]{1,0:T(8,128)(2,1)S(1)}, bf16[144,2048]{1,0:T(8,128)(2,1)S(1)}, u32[]{:S(2)}, u32[]{:S(2)}) %collective-permute-start.14) | collective-permute-done | bytes 589856 | tf_op jit(solution)/shard_map/ppermute | solution.py:61
  111.7 0.3 merge.1.home_ref
  112.1 0.7 collective-permute-start.15
  112.8 0.0 slice-done
  112.8 0.0 slice-done.1
  112.8 1.6 %load_8.1.w_ref = bf16[1024,2048]{1,0:T(8,128)(2,1)S(1)} custom-call(s32[9]{0:T(128)S(1)} %stack.115.info, bf16[1024,4096]{1,0:T(8,128)(2,1)S(1)} %bitcast.26), custom_call_target="tpu_custom_call" | custom-call | bytes 8388608 | tf_op jit(solution)/shard_map/load_8/pallas_call | solution.py:301
  114.4 0.0 collective-permute-done.15.away_ref
  114.4 1.8 %project.2 = (bf16[256,1024]{1,0:T(8,128)(2,1)S(1)}, f32[256,1024]{1,0:T(8,128)S(1)}) custom-call(s32[9]{0:T(128)S(1)} %stack.115.info, bf16[256,1024]{1,0:T(8,128)(2,1)S(1)} %merge.1.home_ref, bf16[256,1024]{1,0:T(8,128)(2,1)S(1)} %collective-permute-done.15.away_ref, bf16[1024,2048]{1,0:T(8,128)(2,1)S(1)} %load_8.1.w_ref), custom_call_target="tpu_custom_call" | custom-call | tf_op jit(solution)/shard_map/project/pallas_call | solution.py:328
  116.3 10.5 %collective-permute-start.16 = (bf16[256,1024]{1,0:T(8,128)(2,1)S(1)}, bf16[256,1024]{1,0:T(8,128)(2,1)S(1)}, u32[]{:S(2)}, u32[]{:S(2)}) collective-permute-start(bf16[256,1024]{1,0:T(8,128)(2,1)S(1)} %get-tuple-element.43), channel_id=1, source_target_pairs={{0,1},{1,0},{2,3},{3,2},{4,5},{5,4},{6,7},{7,6},{8,9},{9,8},{10,11... | collective-permute-start | bytes 1572872 | tf_op jit(solution)/shard_map/ppermute | solution.py:61
  126.8 1.5 %collective-permute-done.16 = bf16[256,1024]{1,0:T(8,128)(2,1)S(1)} collective-permute-done((bf16[256,1024]{1,0:T(8,128)(2,1)S(1)}, bf16[256,1024]{1,0:T(8,128)(2,1)S(1)}, u32[]{:S(2)}, u32[]{:S(2)}) %collective-permute-start.16) | collective-permute-done | bytes 524320 | tf_op jit(solution)/shard_map/ppermute | solution.py:61
  128.3 0.1 add_convert_fusion.1
  128.5 0.1 collective-permute-start.18
  128.6 1.6 %load_7.1.w_ref = bf16[1024,2048]{1,0:T(8,128)(2,1)S(1)} custom-call(s32[9]{0:T(128)S(1)} %stack.115.info, bf16[1024,4096]{1,0:T(8,128)(2,1)S(1)} %bitcast.26), custom_call_target="tpu_custom_call" | custom-call | bytes 8388608 | tf_op jit(solution)/shard_map/load_7/pallas_call | solution.py:301
  130.2 1.8 %project.3 = (bf16[256,1024]{1,0:T(8,128)(2,1)S(1)}, f32[256,1024]{1,0:T(8,128)S(1)}) custom-call(s32[9]{0:T(128)S(1)} %stack.115.info, bf16[256,1024]{1,0:T(8,128)(2,1)S(1)} %merge.1.home_ref, bf16[256,1024]{1,0:T(8,128)(2,1)S(1)} %collective-permute-done.15.away_ref, bf16[1024,2048]{1,0:T(8,128)(2,1)S(1)} %load_7.1.w_ref), custom_call_target="tpu_custom_call" | custom-call | tf_op jit(solution)/shard_map/project/pallas_call | solution.py:328
  132.0 0.5 collective-permute-start.17
  132.5 11.8 %collective-permute-done.18 = bf16[256,1024]{1,0:T(8,128)(2,1)S(1)} collective-permute-done((bf16[256,1024]{1,0:T(8,128)(2,1)S(1)}, bf16[256,1024]{1,0:T(8,128)(2,1)S(1)}, u32[]{:S(2)}, u32[]{:S(2)}) %collective-permute-start.18) | collective-permute-done | bytes 524320 | tf_op jit(solution)/shard_map/ppermute | solution.py:61
  144.3 0.0 collective-permute-done.17
  144.3 1.0 add_convert_fusion
  (7 shorter events, 0.2 us)
Async XLA Ops:
  1.6 1.6 %collective-permute-start = (bf16[512,128]{1,0:T(8,128)(2,1)}, bf16[512,128]{1,0:T(8,128)(2,1)S(1)}, u32[]{:S(2)}, u32[]{:S(2)}) collective-permute-start(bf16[512,128]{1,0:T(8,128)(2,1)} %pack.1), channel_id=1, source_target_pairs={{0,0},{1,32},{2,2},{3,34},{4,4},{5,36},{6,6},{7,38},{8,8},{9,40},{... | collective-permute-start | bytes 393224 | tf_op jit(solution)/shard_map/ppermute | solution.py:61
  3.2 6.0 %collective-permute-start.3 = (bf16[512,128]{1,0:T(8,128)(2,1)S(1)}, bf16[512,128]{1,0:T(8,128)(2,1)S(1)}, u32[]{:S(2)}, u32[]{:S(2)}) collective-permute-start(bf16[512,128]{1,0:T(8,128)(2,1)S(1)} %collective-permute-done), channel_id=1, source_target_pairs={{0,8},{1,25},{2,10},{3,27},{4,28},{5,13},{6,30},{7,15},{8,16},{9,1... | collective-permute-start | bytes 393224 | tf_op jit(solution)/shard_map/ppermute | solution.py:61
  3.2 6.4 %collective-permute-start.2 = (bf16[512,128]{1,0:T(8,128)(2,1)S(1)}, bf16[512,128]{1,0:T(8,128)(2,1)S(1)}, u32[]{:S(2)}, u32[]{:S(2)}) collective-permute-start(bf16[512,128]{1,0:T(8,128)(2,1)S(1)} %collective-permute-done), channel_id=1, source_target_pairs={{0,28},{1,5},{2,30},{3,7},{4,8},{5,1},{6,10},{7,3},{8,4},{9,13},{1... | collective-permute-start | bytes 393224 | tf_op jit(solution)/shard_map/ppermute | solution.py:61
  4.7 5.3 %collective-permute-start.1 = (bf16[512,128]{1,0:T(8,128)(2,1)S(1)}, bf16[512,128]{1,0:T(8,128)(2,1)S(1)}, u32[]{:S(2)}, u32[]{:S(2)}) collective-permute-start(bf16[512,128]{1,0:T(8,128)(2,1)S(1)} %collective-permute-done), channel_id=1, source_target_pairs={{0,4},{1,29},{2,6},{3,31},{4,0},{5,9},{6,2},{7,11},{8,12},{9,5},{1... | collective-permute-start | bytes 393224 | tf_op jit(solution)/shard_map/ppermute | solution.py:61
  10.1 14.3 %collective-permute-start.6 = (bf16[2048,128]{1,0:T(8,128)(2,1)S(1)}, bf16[2048,128]{1,0:T(8,128)(2,1)S(1)}, u32[]{:S(2)}, u32[]{:S(2)}) collective-permute-start(bf16[2048,128]{1,0:T(8,128)(2,1)S(1)} %get-tuple-element.50.refs_0_), channel_id=1, source_target_pairs={{0,192},{1,65},{2,194},{3,67},{4,196},{5,69},{6,198},{7,71},{8,200... | collective-permute-start | bytes 1572872 | tf_op jit(solution)/shard_map/ppermute | solution.py:61
  13.2 14.4 %collective-permute-start.5 = (bf16[2048,128]{1,0:T(8,128)(2,1)S(1)}, bf16[2048,128]{1,0:T(8,128)(2,1)S(1)}, u32[]{:S(2)}, u32[]{:S(2)}) collective-permute-start(bf16[2048,128]{1,0:T(8,128)(2,1)S(1)} %get-tuple-element.50.refs_0_), channel_id=1, source_target_pairs={{0,64},{1,193},{2,66},{3,195},{4,68},{5,197},{6,70},{7,199},{8,72}... | collective-permute-start | bytes 1572872 | tf_op jit(solution)/shard_map/ppermute | solution.py:61
  13.4 14.3 %collective-permute-start.4 = (bf16[2048,128]{1,0:T(8,128)(2,1)S(1)}, bf16[2048,128]{1,0:T(8,128)(2,1)S(1)}, u32[]{:S(2)}, u32[]{:S(2)}) collective-permute-start(bf16[2048,128]{1,0:T(8,128)(2,1)S(1)} %bitcast.28), channel_id=1, source_target_pairs={{0,0},{1,224},{2,2},{3,226},{4,4},{5,228},{6,6},{7,230},{8,8},{9,2... | collective-permute-start | bytes 1572872 | tf_op jit(solution)/shard_map/ppermute | solution.py:61
  14.1 7.2 %collective-permute-start.7 = (bf16[1024,128]{1,0:T(8,128)(2,1)S(1)}, bf16[1024,128]{1,0:T(8,128)(2,1)S(1)}, u32[]{:S(2)}, u32[]{:S(2)}) collective-permute-start(bf16[1024,128]{1,0:T(8,128)(2,1)S(1)} %get-tuple-element.49), channel_id=1, source_target_pairs={{0,4},{1,29},{2,6},{3,31},{4,0},{5,9},{6,2},{7,11},{8,12},{9,5},{1... | collective-permute-start | bytes 786440 | tf_op jit(solution)/shard_map/ppermute | solution.py:61
  16.9 7.5 %collective-permute-start.8 = (bf16[1024,128]{1,0:T(8,128)(2,1)S(1)}, bf16[1024,128]{1,0:T(8,128)(2,1)S(1)}, u32[]{:S(2)}, u32[]{:S(2)}) collective-permute-start(bf16[1024,128]{1,0:T(8,128)(2,1)S(1)} %get-tuple-element.49), channel_id=1, source_target_pairs={{0,8},{1,25},{2,10},{3,27},{4,28},{5,13},{6,30},{7,15},{8,16},{9,1... | collective-permute-start | bytes 786440 | tf_op jit(solution)/shard_map/ppermute | solution.py:61
  27.7 10.4 %collective-permute-start.9 = (bf16[2048,128]{1,0:T(8,128)(2,1)S(1)}, bf16[2048,128]{1,0:T(8,128)(2,1)S(1)}, u32[]{:S(2)}, u32[]{:S(2)}) collective-permute-start(bf16[2048,128]{1,0:T(8,128)(2,1)S(1)} %collective-permute-done.4), channel_id=1, source_target_pairs={{0,1},{1,0},{2,3},{3,2},{4,5},{5,4},{6,7},{7,6},{8,9},{9,8},{10,11... | collective-permute-start | bytes 1572872 | tf_op jit(solution)/shard_map/ppermute | solution.py:61
  34.3 18.6 %collective-permute-start.12 = (bf16[2048,128]{1,0:T(8,128)(2,1)S(1)}, bf16[2048,128]{1,0:T(8,128)(2,1)S(1)}, u32[]{:S(2)}, u32[]{:S(2)}) collective-permute-start(bf16[2048,128]{1,0:T(8,128)(2,1)S(1)} %constant_dynamic-update-slice_fusion.6.refs_3_), channel_id=1, source_target_pairs={{0,192},{1,65},{2,194},{3,67},{4,196},{5,69},{6,198},{7,71},{8,200... | collective-permute-start | bytes 1572872 | tf_op jit(solution)/shard_map/ppermute | solution.py:61
  36.9 15.1 %collective-permute-start.11 = (bf16[2048,128]{1,0:T(8,128)(2,1)S(1)}, bf16[2048,128]{1,0:T(8,128)(2,1)S(1)}, u32[]{:S(2)}, u32[]{:S(2)}) collective-permute-start(bf16[2048,128]{1,0:T(8,128)(2,1)S(1)} %constant_dynamic-update-slice_fusion.6.refs_3_), channel_id=1, source_target_pairs={{0,64},{1,193},{2,66},{3,195},{4,68},{5,197},{6,70},{7,199},{8,72}... | collective-permute-start | bytes 1572872 | tf_op jit(solution)/shard_map/ppermute | solution.py:61
  37.3 18.4 %collective-permute-start.10 = (bf16[2048,128]{1,0:T(8,128)(2,1)S(1)}, bf16[2048,128]{1,0:T(8,128)(2,1)S(1)}, u32[]{:S(2)}, u32[]{:S(2)}) collective-permute-start(bf16[2048,128]{1,0:T(8,128)(2,1)S(1)} %collective-permute-done.5.refs_1_), channel_id=1, source_target_pairs={{0,192},{1,65},{2,194},{3,67},{4,196},{5,69},{6,198},{7,71},{8,200... | collective-permute-start | bytes 1572872 | tf_op jit(solution)/shard_map/ppermute | solution.py:61
  38.1 74.7 %slice-start = ((s8[8388608]{0:T(1024)(128)(4,1)}), s8[4194304]{0:T(1024)(128)(4,1)S(1)}, s32[]{:S(2)}) async-start(s8[8388608]{0:T(1024)(128)(4,1)} %bitcast.25), calls=%async_computation | async-start | bytes 8388608
  52.0 60.8 %slice-start.1 = ((s8[8388608]{0:T(1024)(128)(4,1)}), s8[4194304]{0:T(1024)(128)(4,1)S(1)}, s32[]{:S(2)}) async-start(s8[8388608]{0:T(1024)(128)(4,1)} %bitcast.25), calls=%async_computation.1 | async-start | bytes 8388608
  52.0 10.7 %collective-permute-start.13 = (bf16[2048,128]{1,0:T(8,128)(2,1)S(1)}, bf16[2048,128]{1,0:T(8,128)(2,1)S(1)}, u32[]{:S(2)}, u32[]{:S(2)}) collective-permute-start(bf16[2048,128]{1,0:T(8,128)(2,1)S(1)} %collective-permute-done.11.refs_1_.refs_5_), channel_id=1, source_target_pairs={{0,192},{1,65},{2,194},{3,67},{4,196},{5,69},{6,198},{7,71},{8,200... | collective-permute-start | bytes 1572872 | tf_op jit(solution)/shard_map/ppermute | solution.py:61
  109.7 2.1 %collective-permute-start.14 = (bf16[144,2048]{1,0:T(8,128)(2,1)S(1)}, bf16[144,2048]{1,0:T(8,128)(2,1)S(1)}, u32[]{:S(2)}, u32[]{:S(2)}) collective-permute-start(bf16[144,2048]{1,0:T(8,128)(2,1)S(1)} %get-tuple-element.39), channel_id=1, source_target_pairs={{0,1},{1,0},{2,3},{3,2},{4,5},{5,4},{6,7},{7,6},{8,9},{9,8},{10,11... | collective-permute-start | bytes 1769480 | tf_op jit(solution)/shard_map/ppermute | solution.py:61
  112.1 2.3 %collective-permute-start.15 = (bf16[256,1024]{1,0:T(8,128)(2,1)S(1)}, bf16[256,1024]{1,0:T(8,128)(2,1)S(1)}, u32[]{:S(2)}, u32[]{:S(2)}) collective-permute-start(bf16[256,1024]{1,0:T(8,128)(2,1)S(1)} %merge.1.home_ref), channel_id=1, source_target_pairs={{1,224},{3,226},{5,228},{7,230},{9,232},{11,234},{13,236},{15,238}... | collective-permute-start | bytes 1572872 | tf_op jit(solution)/shard_map/ppermute | solution.py:61
  116.3 12.1 %collective-permute-start.16 = (bf16[256,1024]{1,0:T(8,128)(2,1)S(1)}, bf16[256,1024]{1,0:T(8,128)(2,1)S(1)}, u32[]{:S(2)}, u32[]{:S(2)}) collective-permute-start(bf16[256,1024]{1,0:T(8,128)(2,1)S(1)} %get-tuple-element.43), channel_id=1, source_target_pairs={{0,1},{1,0},{2,3},{3,2},{4,5},{5,4},{6,7},{7,6},{8,9},{9,8},{10,11... | collective-permute-start | bytes 1572872 | tf_op jit(solution)/shard_map/ppermute | solution.py:61
  128.5 15.8 %collective-permute-start.18 = (bf16[256,1024]{1,0:T(8,128)(2,1)S(1)}, bf16[256,1024]{1,0:T(8,128)(2,1)S(1)}, u32[]{:S(2)}, u32[]{:S(2)}) collective-permute-start(bf16[256,1024]{1,0:T(8,128)(2,1)S(1)} %add_convert_fusion.1), channel_id=1, source_target_pairs={{0,2},{1,3},{2,0},{3,1},{4,6},{5,7},{6,4},{7,5},{8,10},{9,11},{10,... | collective-permute-start | bytes 1572872 | tf_op jit(solution)/shard_map/ppermute | solution.py:61
  132.0 12.3 %collective-permute-start.17 = (bf16[256,1024]{1,0:T(8,128)(2,1)S(1)}, bf16[256,1024]{1,0:T(8,128)(2,1)S(1)}, u32[]{:S(2)}, u32[]{:S(2)}) collective-permute-start(bf16[256,1024]{1,0:T(8,128)(2,1)S(1)} %get-tuple-element.47), channel_id=1, source_target_pairs={{0,1},{1,0},{2,3},{3,2},{4,5},{5,4},{6,7},{7,6},{8,9},{9,8},{10,11... | collective-permute-start | bytes 1572872 | tf_op jit(solution)/shard_map/ppermute | solution.py:61
